TPU v7x, 128 devices: a whole 4x4x4 slice. The times are simulated.
128 devices in a mesh: seq: 16 (over y, x), mp: 8 (over z, core).
Axes of the slice: x: 4, y: 4, z: 4, core: 2. Of those that a mesh axis runs over, the one named last changes fastest.
Arguments:
- residual_activations: bfloat16 [16384, 4096], P('seq', 'mp'), may hold values from -6 to 6
- prelayer_gain_vector: bfloat16 [4096], replicated, may hold values from 0.099609375 to 1.8984375
- gating_projection: bfloat16 [4096], replicated, may hold values from -0.25 to 0.25
- asker_projection: bfloat16 [4096, 8192], P(None, 'mp'), may hold values from -0.09375 to 0.09375
- lookup_projection: bfloat16 [4096, 1024], P(None, 'mp'), may hold values from -0.09375 to 0.09375
- content_projection: bfloat16 [4096, 1024], P(None, 'mp'), may hold values from -0.09375 to 0.09375
- final_projection: bfloat16 [8192, 4096], P(None, 'mp'), may hold values from -0.0625 to 0.0625
- logit_sharpness: float32 [64], P('mp'), may hold values from 1 to 64
- selection_table: int32 [16, 256], P('seq'), may hold values from 0 to 1023, as said below
- dispatched_tally_table: int32 [16, 16], replicated, may hold values from 0 to 16, as said below
Outputs:
- blended: bfloat16 [16384, 4096], P('seq', 'mp')
Inputs may be any that keep to these rules, and one draw needn't show every extreme that they name: `dispatched_tally_table`: entry [s, d] counts the routed tokens of source shard s whose compacted place falls to owner d: the compacted sequence lists all routed tokens in sequence order and is dealt in blocks of 8 places, block b to owner b mod 16. Every entry is a multiple of 8, and every column sums to 128. `selection_table`: row s lists in increasing order the distinct local indices of the routed tokens of source shard s, as many as row s of dispatched_tally_table sums to, and zeros after them.
All inputs are finite; a program needn't handle non-finite values.
Results may differ from a plain program's by a relative error of at most 0.0059.
Values may be sent and summed in bfloat16 or wider, within the bound.
No kernel may reach another device: no remote copies, remote signals or barrier semaphores. Data moves between devices by JAX's collectives and lax.ppermute only.
A program may use at most 64 MiB of HBM per device.

v0:
```python
import math
import jax
import jax.numpy as jnp
from jax import lax
from jax.sharding import PartitionSpec as P

HEADS = 64
SHARED_KV_COUNT = 8
PER_HEAD_DIM = 128
SEL = 128


def compact(incoming, prefix, spans, shard, nseq, owned):
    span_ids = jnp.arange(nseq, dtype=jnp.int32) * nseq + shard
    source_of = jnp.sum(
        (prefix[None, :] + spans[None, :] <= span_ids[:, None]).astype(jnp.int32), axis=1
    )
    matches = source_of[:, None] == jnp.arange(nseq, dtype=jnp.int32)[None, :]
    start_of = jnp.sum(jnp.where(matches, prefix[None, :], 0), axis=1)
    half_of = (span_ids - start_of) // nseq
    blocks = incoming.reshape(2 * nseq, incoming.shape[2], incoming.shape[3])
    return blocks[half_of * nseq + source_of].reshape(owned, incoming.shape[3])


def build_return(delta, prefix, spans, shard, nseq, block_rows):
    first = (shard - prefix) % nseq
    counter = jnp.arange(2, dtype=jnp.int32)[:, None] * nseq + first[None, :]
    usable = counter < spans[None, :]
    target = jnp.minimum((prefix[None, :] + counter) // nseq, nseq - 1)
    blocks = delta.reshape(nseq, block_rows, delta.shape[1])[target]
    return jnp.where(usable[:, :, None, None], blocks, jnp.zeros_like(blocks))


def on_device(
    residual_activations,
    prelayer_gain_vector,
    gating_projection,
    asker_projection,
    lookup_projection,
    content_projection,
    final_projection,
    logit_sharpness,
    selection_table,
    dispatched_tally_table,
):
    nseq = lax.axis_size("seq")
    shard = lax.axis_index("seq")
    owned = SEL
    block_rows = owned // nseq
    slots = selection_table.shape[1]
    sent = jnp.sum(dispatched_tally_table, axis=1)
    spans = sent // block_rows
    prefix = jnp.cumsum(spans) - spans
    mine = jnp.arange(nseq, dtype=jnp.int32) == shard
    my_prefix = jnp.sum(jnp.where(mine, prefix, 0))
    my_sent = jnp.sum(jnp.where(mine, sent, 0))
    rotation = my_prefix % nseq
    index_list = selection_table[0]
    live = jnp.arange(slots) < my_sent
    gathered_rows = residual_activations[index_list]
    gathered_rows = jnp.where(live[:, None], gathered_rows, jnp.zeros_like(gathered_rows))
    whole_rows = lax.all_gather(gathered_rows, "mp", axis=1, tiled=True)
    outgoing = jnp.roll(
        whole_rows.reshape(2, nseq, block_rows, whole_rows.shape[1]), rotation, axis=1
    )
    incoming = lax.all_to_all(outgoing, "seq", split_axis=1, concat_axis=1, tiled=True)
    full = compact(incoming, prefix, spans, shard, nseq, owned)
    gate = jax.nn.sigmoid(jnp.dot(full, gating_projection, preferred_element_type=jnp.float32))
    widened = full.astype(jnp.float32)
    inverse = lax.rsqrt(jnp.mean(widened * widened, axis=1, keepdims=True) + 1e-05)
    normed = (widened * inverse * prelayer_gain_vector.astype(jnp.float32)).astype(jnp.bfloat16)
    query = jnp.dot(normed, asker_projection, preferred_element_type=jnp.float32).astype(
        jnp.bfloat16
    )
    keys = jnp.dot(normed, lookup_projection, preferred_element_type=jnp.float32).astype(
        jnp.bfloat16
    )
    values = jnp.dot(normed, content_projection, preferred_element_type=jnp.float32).astype(
        jnp.bfloat16
    )
    paired = jnp.stack([keys, values])
    memory_pair_portion = lookup_projection.shape[1] // PER_HEAD_DIM
    asker_cluster = HEADS // SHARED_KV_COUNT
    query_heads = query.reshape(owned, memory_pair_portion, asker_cluster, PER_HEAD_DIM)
    gating_multipliers = logit_sharpness.reshape(memory_pair_portion, asker_cluster) / math.sqrt(
        PER_HEAD_DIM
    )
    own_slots = jnp.arange(owned, dtype=jnp.int32)
    query_places = (
        own_slots // block_rows * nseq * block_rows + shard * block_rows + own_slots % block_rows
    )
    start_best = jnp.full((memory_pair_portion, asker_cluster, owned), -1e30, jnp.float32)
    piece = lax.all_gather(paired, "seq", axis=1, tiled=True)
    best = start_best
    count = piece.shape[1]
    key_piece = piece[0].reshape(count, memory_pair_portion, PER_HEAD_DIM)
    value_piece = piece[1].reshape(count, memory_pair_portion, PER_HEAD_DIM)
    index_all = jnp.arange(count, dtype=jnp.int32)
    owner = index_all // owned
    position = index_all % owned
    key_places = (
        position // block_rows * nseq * block_rows + owner * block_rows + position % block_rows
    )
    allowed = key_places[None, :] <= query_places[:, None]
    score = jnp.einsum("qngd,knd->ngqk", query_heads, key_piece, preferred_element_type=jnp.float32)
    score = jnp.where(allowed[None, None], score * gating_multipliers[:, :, None, None], -1e30)
    new_best = jnp.maximum(best, jnp.max(score, axis=3))
    weights = jnp.where(allowed[None, None], jnp.exp(score - new_best[..., None]), 0.0)
    totals = jnp.sum(weights, axis=3)
    mixed = jnp.einsum(
        "ngqk,knd->ngqd",
        weights.astype(jnp.bfloat16),
        value_piece,
        preferred_element_type=jnp.float32,
    )
    sums = mixed
    best, totals, sums = (new_best, totals, sums)
    attended = (sums / totals[..., None]).astype(jnp.bfloat16)
    attended = attended.transpose(2, 0, 1, 3).reshape(
        owned, memory_pair_portion * asker_cluster * PER_HEAD_DIM
    )
    projected = jnp.dot(
        lax.all_gather(attended, "mp", axis=1, tiled=True),
        final_projection,
        preferred_element_type=jnp.float32,
    )
    delta = (gate[:, None] * projected).astype(jnp.bfloat16)
    outgoing_back = build_return(delta, prefix, spans, shard, nseq, block_rows)
    coming_back = lax.all_to_all(outgoing_back, "seq", split_axis=1, concat_axis=1, tiled=True)
    restored = jnp.roll(coming_back, -rotation, axis=1).reshape(slots, delta.shape[1])
    restored = jnp.where(live[:, None], restored, jnp.zeros_like(restored))
    updated = (
        residual_activations.astype(jnp.float32).at[index_list].add(restored.astype(jnp.float32))
    )
    return updated.astype(jnp.bfloat16)


def solution(mesh):
    placed = (
        P("seq", "mp"),
        P(),
        P(),
        P(None, "mp"),
        P(None, "mp"),
        P(None, "mp"),
        P(None, "mp"),
        P("mp"),
        P("seq", None),
        P(),
    )
    return jax.shard_map(
        on_device, mesh=mesh, in_specs=placed, out_specs=P("seq", "mp"), check_vma=False
    )
```

profile of v0, /device:TPU:1, one launch (start us, length us, event | category | flops | bytes accessed | tf_op | source)
XLA Modules:
  0.0 201.7 jit_solution(617594323271170253)
XLA Ops:
  6.5 0.9 reduce_sum.69
  7.7 0.6 and_select_fusion.4
  8.3 0.6 iota_compare_fusion.1
  9.0 0.7 compare_select_fusion
  9.7 2.6 %gather_fusion = bf16[256,512]{1,0:T(8,128)(2,1)S(1)} fusion(bf16[1024,512]{1,0:T(8,128)(2,1)} %param.10, s32[1024]{0:T(1024)S(1)} %pad_clamp_fusion.2), kind=kCustom, calls=%fused_computation | custom fusion | bytes 525312 | tf_op jit(solution)/shard_map/gather | solution.py:60
  12.3 0.8 broadcast_select_fusion
  13.1 0.6 fusion.52
  15.6 26.6 %all-gather.4.cloned.1.call-done = bf16[256,4096]{1,0:T(8,128)(2,1)} async-done(((bf16[256,512]{1,0:T(8,128)(2,1)}), bf16[256,4096]{1,0:T(8,128)(2,1)}) %all-gather.4.cloned.1.call-update) | async-done | bytes 2097168 | tf_op jit(solution)/shard_map/all_gather | solution.py:62
  42.3 2.4 %fusion.7 = bf16[2,16,8,4096]{3,2,1,0:T(8,128)(2,1)S(1)} fusion(s32[]{:T(128)S(6)} %select_n.208, bf16[2,16,8,4096]{3,2,1,0:T(8,128)(2,1)} %bitcast.124), kind=kLoop, calls=%fused_computation.15 | loop fusion | flops 1048576 | bytes 4194308 | tf_op jit(solution)/shard_map/jit(_roll_dynamic)/concatenate | solution.py:63
  44.6 1.5 copy.48
  46.1 6.6 %all-to-all-start = ((bf16[2,16,8,4096]{3,2,0,1:T(8,128)(2,1)}), bf16[2,16,8,4096]{3,2,0,1:T(8,128)(2,1)S(1)}, u32[]{:S(2)}, u32[]{:S(2)}) async-start(bf16[2,16,8,4096]{3,2,0,1:T(8,128)(2,1)} %copy.48), calls=%async_computation | async-start | bytes 4194304 | tf_op jit(solution)/shard_map/all_to_all | solution.py:66
  53.2 32.2 %all-to-all-done = bf16[2,16,8,4096]{3,2,0,1:T(8,128)(2,1)S(1)} async-done(((bf16[2,16,8,4096]{3,2,0,1:T(8,128)(2,1)}), bf16[2,16,8,4096]{3,2,0,1:T(8,128)(2,1)S(1)}, u32[]{:S(2)}, u32[]{:S(2)}) %all-to-all-start) | async-done | bytes 2097184 | tf_op jit(solution)/shard_map/all_to_all | solution.py:66
  85.4 1.5 copy.38
  86.9 2.2 %gather_fusion.1 = bf16[16,8,4096]{2,1,0:T(8,128)(2,1)S(1)} fusion(bf16[32,8,4096]{2,1,0:T(8,128)(2,1)} %bitcast.123, s32[1024]{0:T(1024)S(1)} %pad_clamp_fusion.1), kind=kCustom, calls=%fused_computation.1 | custom fusion | bytes 2097216 | tf_op jit(solution)/shard_map/gather | solution.py:22
  89.5 0.5 fusion.11
  90.0 1.7 fusion.12
  91.8 0.6 pad_maximum_fusion
  92.9 4.7 %fusion.8 = bf16[16,8,8,128]{3,2,1,0:T(8,128)(2,1)S(1)} fusion(bf16[4096,1024]{1,0:T(8,128)(2,1)} %param.13, bf16[16,8,4096]{2,1,0:T(8,128)(2,1)S(1)} %gather_fusion.1, f32[4096]{0:T(1024)S(1)} %convert_element_type.49, f32[128]{0:T(128)S(1)} %rsqrt.12), kind=kOutput, calls=%fused_computation.20 | convolution fusion | flops 1075970048 | bytes 9716224 | tf_op jit(solution)/shard_map/dot_general | solution.py:72
  97.6 34.0 %all-gather.6.cloned.1.call-done = bf16[2,2048,128]{2,1,0:T(8,128)(2,1)} async-done(((bf16[2,128,128]{2,1,0:T(8,128)(2,1)}), bf16[2,2048,128]{2,1,0:T(8,128)(2,1)}) %all-gather.6.cloned.1.call-update) | async-done | bytes 1048592 | tf_op jit(solution)/shard_map/all_gather | solution.py:93
  131.6 2.3 %fusion = (f32[8,128]{1,0:T(8,128)S(1)}, f32[2048,128,8]{1,0,2:T(8,128)S(1)}) fusion(f32[8]{0:T(128)S(1)} %broadcast_multiply_fusion, pred[128,2048]{0,1:T(8,128)(4,1)S(1)} %broadcast_compare_fusion, bf16[16,8,8,128]{3,2,1,0:T(8,128)(2,1)S(1)} %fusion.8, bf16[2,2048,128]{2,1,0:T(8,128)(2,1)} %all-gather.6.cloned.1.call-done), kind=kOutput, calls=%fused_computation.7 | convolution fusion | flops 543161344 | bytes 9441312 | tf_op jit(solution)/shard_map/qngd,knd->ngqk/dot_general | solution.py:105
  133.9 2.1 %fusion.1 = f32[8,128]{1,0:T(8,128)S(1)} fusion(f32[2048,128,8]{1,0,2:T(8,128)S(1)} %get-tuple-element.10, f32[8,128]{1,0:T(8,128)S(1)} %broadcast_maximum_fusion, f32[8]{0:T(128)S(1)} %broadcast_multiply_fusion, pred[128,2048]{0,1:T(8,128)(4,1)S(1)} %broadcast_compare_fusion), kind=kLoop, calls=%fused_computation.8 | loop fusion | flops 10484736 | bytes 8658976 | tf_op jit(solution)/shard_map/reduce_sum | solution.py:109
  136.0 2.8 %fusion.21 = bf16[8,128,128]{1,2,0:T(8,128)(2,1)} fusion(f32[2048,128,8]{1,0,2:T(8,128)S(1)} %get-tuple-element.10, f32[8,128]{1,0:T(8,128)S(1)} %broadcast_maximum_fusion, f32[8]{0:T(128)S(1)} %broadcast_multiply_fusion, pred[128,2048]{0,1:T(8,128)(4,1)S(1)} %broadcast_compare_fusion, bf16[2,2048,128]{2,1,0:T(8,128)(2,1)S(1)} %copy-done.2, ...), kind=kOutput, calls=%fused_computation.34 | convolution fusion | flops 547618816 | bytes 9445888 | tf_op jit(solution)/shard_map/ngqk,knd->ngqd/dot_general | solution.py:110
  139.2 0.4 fusion.16
  139.5 26.0 %all-gather.8.cloned.1.call-done = bf16[128,8192]{0,1:T(8,128)(2,1)} async-done(((bf16[128,1024]{0,1:T(8,128)(2,1)}), bf16[128,8192]{0,1:T(8,128)(2,1)}) %all-gather.8.cloned.1.call-update) | async-done | bytes 2097168 | tf_op jit(solution)/shard_map/all_gather | solution.py:123
  165.5 5.3 %fusion.10 = bf16[16,8,512]{2,1,0:T(8,128)(2,1)S(1)} fusion(bf16[128,8192]{0,1:T(8,128)(2,1)} %all-gather.8.cloned.1.call-done, bf16[8192,512]{1,0:T(8,128)(2,1)} %param.16, f32[128]{0:T(128)S(1)} %fusion.16), kind=kOutput, calls=%fused_computation.22 | convolution fusion | flops 1073872896 | bytes 10617344 | tf_op jit(solution)/shard_map/dot_general | solution.py:122
  170.9 0.6 gather_fusion.2
  171.5 0.7 copy.42
  172.3 6.5 %all-to-all-start.1 = ((bf16[2,16,8,512]{3,2,0,1:T(8,128)(2,1)}), bf16[2,16,8,512]{3,2,0,1:T(8,128)(2,1)S(1)}, u32[]{:S(2)}, u32[]{:S(2)}) async-start(bf16[2,16,8,512]{3,2,0,1:T(8,128)(2,1)} %copy.42), calls=%async_computation.1 | async-start | bytes 524288 | tf_op jit(solution)/shard_map/all_to_all | solution.py:129
  178.8 1.6 convert_element_type.45
  180.5 6.6 %all-to-all-done.1 = bf16[2,16,8,512]{3,2,0,1:T(8,128)(2,1)S(1)} async-done(((bf16[2,16,8,512]{3,2,0,1:T(8,128)(2,1)}), bf16[2,16,8,512]{3,2,0,1:T(8,128)(2,1)S(1)}, u32[]{:S(2)}, u32[]{:S(2)}) %all-to-all-start.1) | async-done | bytes 262176 | tf_op jit(solution)/shard_map/all_to_all | solution.py:129
  187.3 5.2 %scatter_custom_fusion = f32[1024,512]{1,0:T(8,128)} fusion(f32[1024,512]{1,0:T(8,128)} %convert_element_type.45, s32[256]{0:T(256)S(1)} %bitcast.128, bf16[256,512]{1,0:T(8,128)(2,1)S(1)} %bitcast_select_fusion.1), kind=kCustom, calls=%fused_computation.40 | custom fusion | flops 262144 | bytes 2359296 | tf_op jit(solution)/shard_map/scatter-add | solution.py:133
  192.5 2.7 %convert_element_type.59 = bf16[1024,512]{1,0:T(8,128)(2,1)} convert(f32[1024,512]{1,0:T(8,128)} %scatter_custom_fusion) | non-fusion elementwise | flops 524288 | bytes 3145728 | tf_op jit(solution)/shard_map/convert_element_type | solution.py:135
  (46 shorter events, 2.2 us)
Async XLA Ops:
  6.5 82.9 %copy-start = (bf16[4096,128]{1,0:T(8,128)(2,1)S(1)}, bf16[4096,128]{1,0:T(8,128)(2,1)}, u32[]{:S(2)}) copy-start(bf16[4096,128]{1,0:T(8,128)(2,1)} %param.14) | copy-start | bytes 3145732
  6.5 35.7 %all-gather.4.cloned.1.call-start = ((), (), s32[]{:S(2)}) async-start(), calls=%async_computation.2 | async-start | bytes 2359296 | tf_op jit(solution)/shard_map/all_gather | solution.py:62
  46.1 6.7 %copy-start.3 = (bf16[4096]{0:T(1024)(128)(2,1)S(1)}, bf16[4096]{0:T(1024)(128)(2,1)}, u32[]{:S(2)}) copy-start(bf16[4096]{0:T(1024)(128)(2,1)} %param.11) | copy-start | bytes 24580
  46.1 39.3 %all-to-all-start = ((bf16[2,16,8,4096]{3,2,0,1:T(8,128)(2,1)}), bf16[2,16,8,4096]{3,2,0,1:T(8,128)(2,1)S(1)}, u32[]{:S(2)}, u32[]{:S(2)}) async-start(bf16[2,16,8,4096]{3,2,0,1:T(8,128)(2,1)} %copy.48), calls=%async_computation | async-start | bytes 4194304 | tf_op jit(solution)/shard_map/all_to_all | solution.py:66
  52.8 78.8 %all-gather.6.cloned.1.call-start = ((), (), s32[]{:S(2)}) async-start(), calls=%async_computation.3 | async-start | bytes 1114112 | tf_op jit(solution)/shard_map/all_gather | solution.py:93
  90.0 2.5 %copy-start.5 = (f32[8]{0:T(128)S(1)}, f32[8]{0:T(128)}, u32[]{:S(2)}) copy-start(f32[8]{0:T(128)} %param.17) | copy-start | bytes 100
  92.4 73.1 %all-gather.8.cloned.1.call-start = ((), (), s32[]{:S(2)}) async-start(), calls=%async_computation.4 | async-start | bytes 2359296 | tf_op jit(solution)/shard_map/all_gather | solution.py:123
  133.9 2.1 %copy-start.2 = (bf16[2,2048,128]{2,1,0:T(8,128)(2,1)S(1)}, bf16[2,2048,128]{2,1,0:T(8,128)(2,1)}, u32[]{:S(2)}) copy-start(bf16[2,2048,128]{2,1,0:T(8,128)(2,1)} %all-gather.6.cloned.1.call-done) | copy-start | bytes 3145732
  136.0 2.8 %copy-start.4 = (bf16[4096]{0:T(1024)(128)(2,1)S(1)}, bf16[4096]{0:T(1024)(128)(2,1)}, u32[]{:S(2)}) copy-start(bf16[4096]{0:T(1024)(128)(2,1)} %param.12) | copy-start | bytes 24580
  170.8 8.0 %copy-start.1 = (bf16[1024,512]{1,0:T(8,128)(2,1)S(1)}, bf16[1024,512]{1,0:T(8,128)(2,1)}, u32[]{:S(2)}) copy-start(bf16[1024,512]{1,0:T(8,128)(2,1)} %param.10) | copy-start | bytes 3145732
  172.3 14.8 %all-to-all-start.1 = ((bf16[2,16,8,512]{3,2,0,1:T(8,128)(2,1)}), bf16[2,16,8,512]{3,2,0,1:T(8,128)(2,1)S(1)}, u32[]{:S(2)}, u32[]{:S(2)}) async-start(bf16[2,16,8,512]{3,2,0,1:T(8,128)(2,1)} %copy.42), calls=%async_computation.1 | async-start | bytes 524288 | tf_op jit(solution)/shard_map/all_to_all | solution.py:129
Sparse Core Ops, SparseCore 0:
  13.2 29.0 all-gather.3
  92.5 38.9 all-gather.5
  139.0 26.4 all-gather.7
where the time goes:
time: 202 us
  waiting for transfers between devices  125 us (62%)
  other arithmetic  20.7 us (10%)
  matrix products  17.7 us (9%)
  between operations  15.3 us (8%)
  starting transfers between devices  13.2 us (7%)
  local copies, waits for them, and re-layouts  9.37 us (5%)
    all_gather x1, waiting for transfers between devices, on_device(): piece = lax.all_gather(paired, 'seq', axis=1, tiled=True)  34 us
    all_to_all x1, waiting for transfers between devices, on_device(): lax.all_to_all(outgoing, 'seq', split_axis=1, concat_axis=1, tiled=True)  32.2 us
    all_gather x1, waiting for transfers between devices, on_device(): whole_rows = lax.all_gather(gathered_rows, 'mp', axis=1, tiled=True)  26.6 us
    all_gather x1, waiting for transfers between devices, on_device(): lax.all_gather(attended, 'mp', axis=1, tiled=True)  26 us
    all_to_all x1, starting transfers between devices, on_device(): lax.all_to_all(outgoing, 'seq', split_axis=1, concat_axis=1, tiled=True)  6.64 us
    all_to_all x1, waiting for transfers between devices, on_device(): lax.all_to_all(outgoing_back, 'seq', split_axis=1, concat_axis=1, tiled=T...  6.56 us
    all_to_all x1, starting transfers between devices, on_device(): lax.all_to_all(outgoing_back, 'seq', split_axis=1, concat_axis=1, tiled=T...  6.52 us
    dot_general x1, matrix products, on_device(): jnp.dot(lax.all_gather(attended, 'mp', axis=1, tiled=True), final_project...  5.31 us
  transfers between devices with their start and end apart: 5, of which 5 were waited for; matrix products, arithmetic and copies ran while one was open for 4% of the time, Pallas kernels for 0%

commit v1 on v0

--- a/solution.py
+++ b/solution.py
@@ -8,6 +8,29 @@
 SHARED_KV_COUNT = 8
 PER_HEAD_DIM = 128
 SEL = 128
+
+
+def in_blocks(shard, dim, devices):
+    before, after = (shard.shape[:dim], shard.shape[dim + 1 :])
+    return jnp.moveaxis(shard.reshape(*before, devices, -1, *after), dim, 0)
+
+
+def in_order(tiles, dim):
+    lengths = list(tiles.shape[1:])
+    lengths[dim] *= tiles.shape[0]
+    return jnp.moveaxis(tiles, 0, dim).reshape(lengths)
+
+
+def rotated_exchange(shard, axis, split_dim, concat_dim):
+    size, here = (lax.axis_size(axis), lax.axis_index(axis))
+    blocks = in_blocks(shard, split_dim, size)
+    result = blocks
+    for step in range(1, size):
+        target, source = ((here + step) % size, (here - step) % size)
+        sent = lax.dynamic_index_in_dim(blocks, target, 0)
+        partner_block = lax.ppermute(sent, axis, [(i, (i + step) % size) for i in range(size)])
+        result = lax.dynamic_update_slice_in_dim(result, partner_block, source, axis=0)
+    return in_order(result, concat_dim)
 
 
 def compact(incoming, prefix, spans, shard, nseq, owned):
@@ -126,7 +149,7 @@
     )
     delta = (gate[:, None] * projected).astype(jnp.bfloat16)
     outgoing_back = build_return(delta, prefix, spans, shard, nseq, block_rows)
-    coming_back = lax.all_to_all(outgoing_back, "seq", split_axis=1, concat_axis=1, tiled=True)
+    coming_back = rotated_exchange(outgoing_back, "seq", 1, 1)
     restored = jnp.roll(coming_back, -rotation, axis=1).reshape(slots, delta.shape[1])
     restored = jnp.where(live[:, None], restored, jnp.zeros_like(restored))
     updated = (

time: 202 us -> 216 us (1.069)
  the two profiles are of different devices: /device:TPU:1 before, /device:TPU:6 now
where the time goes in v1:
time: 216 us; the launch traced here: 215 us
  waiting for transfers between devices  119 us (55%)
  starting transfers between devices  36.3 us (17%)
  matrix products  17.7 us (8%)
  other arithmetic  16.9 us (8%)
  between operations  16 us (7%)
  local copies, waits for them, and re-layouts  8.88 us (4%)
    all_gather x1, waiting for transfers between devices, on_device(): piece = lax.all_gather(paired, 'seq', axis=1, tiled=True)  36.7 us
    all_to_all x1, waiting for transfers between devices, on_device(): lax.all_to_all(outgoing, 'seq', split_axis=1, concat_axis=1, tiled=True)  29.9 us
    ppermute x15, starting transfers between devices, rotated_exchange(): lax.ppermute(sent, axis, [(i, (i + step) % size) for i in range(size)])  28.6 us
    all_gather x1, waiting for transfers between devices, on_device(): whole_rows = lax.all_gather(gathered_rows, 'mp', axis=1, tiled=True)  25.3 us
    all_gather x1, waiting for transfers between devices, on_device(): lax.all_gather(attended, 'mp', axis=1, tiled=True)  22.4 us
    all_to_all x1, starting transfers between devices, on_device(): lax.all_to_all(outgoing, 'seq', split_axis=1, concat_axis=1, tiled=True)  7.42 us
    dot_general x1, matrix products, on_device(): jnp.dot(lax.all_gather(attended, 'mp', axis=1, tiled=True), final_project...  5.31 us
    ppermute x15, waiting for transfers between devices, rotated_exchange(): lax.ppermute(sent, axis, [(i, (i + step) % size) for i in range(size)])  5.17 us
  transfers between devices with their start and end apart: 19, of which 6 were waited for; matrix products, arithmetic and copies ran while one was open for 4% of the time, Pallas kernels for 0%

profile of v1, /device:TPU:6, one launch (start us, length us, event | category | flops | bytes accessed | tf_op | source)
XLA Modules:
  0.0 215.2 jit_solution(415130816733067745)
XLA Ops:
  6.5 0.9 reduce_sum.69
  9.7 2.6 %gather_fusion = bf16[256,512]{1,0:T(8,128)(2,1)S(1)} fusion(bf16[1024,512]{1,0:T(8,128)(2,1)} %param.10, s32[1024]{0:T(1024)S(1)} %pad_clamp_fusion.2), kind=kCustom, calls=%fused_computation | custom fusion | bytes 525312 | tf_op jit(solution)/shard_map/gather | solution.py:83
  15.7 25.3 %all-gather.4.cloned.1.call-done = bf16[256,4096]{1,0:T(8,128)(2,1)} async-done(((bf16[256,512]{1,0:T(8,128)(2,1)}), bf16[256,4096]{1,0:T(8,128)(2,1)}) %all-gather.4.cloned.1.call-update) | async-done | bytes 2097168 | tf_op jit(solution)/shard_map/all_gather | solution.py:85
  40.9 2.3 %fusion.7 = bf16[2,16,8,4096]{3,2,1,0:T(8,128)(2,1)S(1)} fusion(s32[]{:T(128)S(6)} %select_n.426, bf16[2,16,8,4096]{3,2,1,0:T(8,128)(2,1)} %bitcast.161), kind=kLoop, calls=%fused_computation.15 | loop fusion | flops 1048576 | bytes 4194308 | tf_op jit(solution)/shard_map/jit(_roll_dynamic)/concatenate | solution.py:86
  43.3 1.6 copy.43
  44.8 7.4 %all-to-all-start = ((bf16[2,16,8,4096]{3,2,0,1:T(8,128)(2,1)}), bf16[2,16,8,4096]{3,2,0,1:T(8,128)(2,1)S(1)}, u32[]{:S(2)}, u32[]{:S(2)}) async-start(bf16[2,16,8,4096]{3,2,0,1:T(8,128)(2,1)} %copy.43), calls=%async_computation | async-start | bytes 4194304 | tf_op jit(solution)/shard_map/all_to_all | solution.py:89
  52.7 29.9 %all-to-all-done = bf16[2,16,8,4096]{3,2,0,1:T(8,128)(2,1)S(1)} async-done(((bf16[2,16,8,4096]{3,2,0,1:T(8,128)(2,1)}), bf16[2,16,8,4096]{3,2,0,1:T(8,128)(2,1)S(1)}, u32[]{:S(2)}, u32[]{:S(2)}) %all-to-all-start) | async-done | bytes 2097184 | tf_op jit(solution)/shard_map/all_to_all | solution.py:89
  82.6 1.6 copy.35
  84.2 2.2 %gather_fusion.1 = bf16[16,8,4096]{2,1,0:T(8,128)(2,1)S(1)} fusion(bf16[32,8,4096]{2,1,0:T(8,128)(2,1)} %bitcast.158, s32[1024]{0:T(1024)S(1)} %pad_clamp_fusion.1), kind=kCustom, calls=%fused_computation.1 | custom fusion | bytes 2097216 | tf_op jit(solution)/shard_map/gather | solution.py:45
  87.3 1.7 fusion.12
  90.3 4.7 %fusion.8 = bf16[16,8,8,128]{3,2,1,0:T(8,128)(2,1)S(1)} fusion(bf16[4096,1024]{1,0:T(8,128)(2,1)} %param.13, bf16[16,8,4096]{2,1,0:T(8,128)(2,1)S(1)} %gather_fusion.1, f32[4096]{0:T(1024)S(1)} %convert_element_type.49, f32[128]{0:T(128)S(1)} %rsqrt.12), kind=kOutput, calls=%fused_computation.20 | convolution fusion | flops 1075970048 | bytes 9716224 | tf_op jit(solution)/shard_map/dot_general | solution.py:95
  95.0 36.7 %all-gather.6.cloned.1.call-done = bf16[2,2048,128]{2,1,0:T(8,128)(2,1)} async-done(((bf16[2,128,128]{2,1,0:T(8,128)(2,1)}), bf16[2,2048,128]{2,1,0:T(8,128)(2,1)}) %all-gather.6.cloned.1.call-update) | async-done | bytes 1048592 | tf_op jit(solution)/shard_map/all_gather | solution.py:116
  131.7 2.3 %fusion = (f32[8,128]{1,0:T(8,128)S(1)}, f32[2048,128,8]{1,0,2:T(8,128)S(1)}) fusion(f32[8]{0:T(128)S(1)} %broadcast_multiply_fusion, pred[128,2048]{0,1:T(8,128)(4,1)S(1)} %broadcast_compare_fusion, bf16[16,8,8,128]{3,2,1,0:T(8,128)(2,1)S(1)} %fusion.8, bf16[2,2048,128]{2,1,0:T(8,128)(2,1)} %all-gather.6.cloned.1.call-done), kind=kOutput, calls=%fused_computation.7 | convolution fusion | flops 543161344 | bytes 9441312 | tf_op jit(solution)/shard_map/qngd,knd->ngqk/dot_general | solution.py:128
  134.0 2.1 fusion.1
  136.2 2.8 %fusion.21 = bf16[8,128,128]{1,2,0:T(8,128)(2,1)} fusion(f32[2048,128,8]{1,0,2:T(8,128)S(1)} %get-tuple-element.25, f32[8,128]{1,0:T(8,128)S(1)} %broadcast_maximum_fusion, f32[8]{0:T(128)S(1)} %broadcast_multiply_fusion, pred[128,2048]{0,1:T(8,128)(4,1)S(1)} %broadcast_compare_fusion, bf16[2,2048,128]{2,1,0:T(8,128)(2,1)S(1)} %copy-done.3, ...), kind=kOutput, calls=%fused_computation.34 | convolution fusion | flops 547618816 | bytes 9445888 | tf_op jit(solution)/shard_map/ngqk,knd->ngqd/dot_general | solution.py:133
  139.5 1.6 convert_element_type.45
  141.9 22.4 %all-gather.8.cloned.1.call-done = bf16[128,8192]{0,1:T(8,128)(2,1)} async-done(((bf16[128,1024]{0,1:T(8,128)(2,1)}), bf16[128,8192]{0,1:T(8,128)(2,1)}) %all-gather.8.cloned.1.call-update) | async-done | bytes 2097168 | tf_op jit(solution)/shard_map/all_gather | solution.py:146
  164.3 5.3 %fusion.10 = bf16[16,8,512]{2,1,0:T(8,128)(2,1)S(1)} fusion(bf16[128,8192]{0,1:T(8,128)(2,1)} %all-gather.8.cloned.1.call-done, bf16[8192,512]{1,0:T(8,128)(2,1)} %param.16, f32[128]{0:T(128)S(1)} %fusion.16), kind=kOutput, calls=%fused_computation.22 | convolution fusion | flops 1073872896 | bytes 10617344 | tf_op jit(solution)/shard_map/dot_general | solution.py:145
  170.4 1.5 collective-permute-start
  172.0 2.4 %collective-permute-start.1 = (bf16[1,2,1,8,512]{4,3,0,1,2:T(8,128)(2,1)S(1)}, bf16[1,2,1,8,512]{4,3,0,1,2:T(8,128)(2,1)S(1)}, u32[]{:S(2)}, u32[]{:S(2)}) collective-permute-start(bf16[1,2,1,8,512]{4,3,0,1,2:T(8,128)(2,1)S(1)} %get-tuple-element.21), channel_id=1, source_target_pairs={{0,16},{8,24},{16,32},{24,40},{32,48},{40,56},{48,64},{56,72},{64,... | collective-permute-start | bytes 49160 | tf_op jit(solution)/shard_map/ppermute | solution.py:31
  175.3 1.2 collective-permute-start.3
  176.5 3.8 %collective-permute-start.4 = (bf16[1,2,1,8,512]{4,3,0,1,2:T(8,128)(2,1)S(1)}, bf16[1,2,1,8,512]{4,3,0,1,2:T(8,128)(2,1)S(1)}, u32[]{:S(2)}, u32[]{:S(2)}) collective-permute-start(bf16[1,2,1,8,512]{4,3,0,1,2:T(8,128)(2,1)S(1)} %get-tuple-element.18), channel_id=1, source_target_pairs={{0,40},{8,48},{16,56},{24,64},{32,72},{40,80},{48,88},{56,96},{64,... | collective-permute-start | bytes 49160 | tf_op jit(solution)/shard_map/ppermute | solution.py:31
  180.3 1.8 collective-permute-start.5
  182.1 1.5 collective-permute-start.6
  183.7 2.0 collective-permute-start.7
  185.7 1.9 collective-permute-start.8
  187.6 4.0 %collective-permute-start.9 = (bf16[1,2,1,8,512]{4,3,0,1,2:T(8,128)(2,1)S(1)}, bf16[1,2,1,8,512]{4,3,0,1,2:T(8,128)(2,1)S(1)}, u32[]{:S(2)}, u32[]{:S(2)}) collective-permute-start(bf16[1,2,1,8,512]{4,3,0,1,2:T(8,128)(2,1)S(1)} %get-tuple-element.13), channel_id=1, source_target_pairs={{0,80},{8,88},{16,96},{24,104},{32,112},{40,120},{48,0},{56,8},{64... | collective-permute-start | bytes 49160 | tf_op jit(solution)/shard_map/ppermute | solution.py:31
  192.3 5.9 %collective-permute-start.12 = (bf16[1,2,1,8,512]{4,3,0,1,2:T(8,128)(2,1)S(1)}, bf16[1,2,1,8,512]{4,3,0,1,2:T(8,128)(2,1)S(1)}, u32[]{:S(2)}, u32[]{:S(2)}) collective-permute-start(bf16[1,2,1,8,512]{4,3,0,1,2:T(8,128)(2,1)S(1)} %get-tuple-element.10), channel_id=1, source_target_pairs={{0,104},{8,112},{16,120},{24,0},{32,8},{40,16},{48,24},{56,32},{64... | collective-permute-start | bytes 49160 | tf_op jit(solution)/shard_map/ppermute | solution.py:31
  198.2 0.9 collective-permute-start.14
  199.6 4.7 %collective-permute-done.13 = bf16[1,2,1,8,512]{4,3,0,1,2:T(8,128)(2,1)S(1)} collective-permute-done((bf16[1,2,1,8,512]{4,3,0,1,2:T(8,128)(2,1)S(1)}, bf16[1,2,1,8,512]{4,3,0,1,2:T(8,128)(2,1)S(1)}, u32[]{:S(2)}, u32[]{:S(2)}) %collective-permute-start.13) | collective-permute-done | bytes 16416 | tf_op jit(solution)/shard_map/ppermute | solution.py:31
  204.6 2.9 %scatter_custom_fusion = f32[1024,512]{1,0:T(8,128)S(1)} fusion(f32[1024,512]{1,0:T(8,128)S(1)} %copy-done.2, s32[256]{0:T(256)S(1)} %bitcast.165, bf16[256,512]{1,0:T(8,128)(2,1)S(1)} %bitcast_select_fusion.1), kind=kCustom, calls=%fused_computation.40 | custom fusion | flops 262144 | bytes 2359296 | tf_op jit(solution)/shard_map/scatter-add | solution.py:156
  207.5 1.1 convert_element_type.59
  (91 shorter events, 10.1 us)
Async XLA Ops:
  6.5 80.2 %copy-start = (bf16[4096,128]{1,0:T(8,128)(2,1)S(1)}, bf16[4096,128]{1,0:T(8,128)(2,1)}, u32[]{:S(2)}) copy-start(bf16[4096,128]{1,0:T(8,128)(2,1)} %param.14) | copy-start | bytes 3145732
  6.5 34.4 %all-gather.4.cloned.1.call-start = ((), (), s32[]{:S(2)}) async-start(), calls=%async_computation.1 | async-start | bytes 2359296 | tf_op jit(solution)/shard_map/all_gather | solution.py:85
  44.8 7.5 %copy-start.4 = (bf16[4096]{0:T(1024)(128)(2,1)S(1)}, bf16[4096]{0:T(1024)(128)(2,1)}, u32[]{:S(2)}) copy-start(bf16[4096]{0:T(1024)(128)(2,1)} %param.11) | copy-start | bytes 24580
  44.8 37.8 %all-to-all-start = ((bf16[2,16,8,4096]{3,2,0,1:T(8,128)(2,1)}), bf16[2,16,8,4096]{3,2,0,1:T(8,128)(2,1)S(1)}, u32[]{:S(2)}, u32[]{:S(2)}) async-start(bf16[2,16,8,4096]{3,2,0,1:T(8,128)(2,1)} %copy.43), calls=%async_computation | async-start | bytes 4194304 | tf_op jit(solution)/shard_map/all_to_all | solution.py:89
  52.2 79.5 %all-gather.6.cloned.1.call-start = ((), (), s32[]{:S(2)}) async-start(), calls=%async_computation.2 | async-start | bytes 1114112 | tf_op jit(solution)/shard_map/all_gather | solution.py:116
  87.3 2.7 %copy-start.6 = (f32[8]{0:T(128)S(1)}, f32[8]{0:T(128)}, u32[]{:S(2)}) copy-start(f32[8]{0:T(128)} %param.17) | copy-start | bytes 100
  89.7 74.6 %all-gather.8.cloned.1.call-start = ((), (), s32[]{:S(2)}) async-start(), calls=%async_computation.3 | async-start | bytes 2359296 | tf_op jit(solution)/shard_map/all_gather | solution.py:146
  134.0 2.1 copy-start.3
  136.2 3.3 %copy-start.1 = (bf16[1024,512]{1,0:T(8,128)(2,1)S(1)}, bf16[1024,512]{1,0:T(8,128)(2,1)}, u32[]{:S(2)}) copy-start(bf16[1024,512]{1,0:T(8,128)(2,1)} %param.10) | copy-start | bytes 3145732
  139.0 2.1 copy-start.5
  169.6 35.0 %copy-start.2 = (f32[1024,512]{1,0:T(8,128)S(1)}, f32[1024,512]{1,0:T(8,128)}, u32[]{:S(2)}) copy-start(f32[1024,512]{1,0:T(8,128)} %convert_element_type.45) | copy-start | bytes 6291460
  170.4 10.0 %collective-permute-start = (bf16[1,2,1,8,512]{4,3,0,1,2:T(8,128)(2,1)S(1)}, bf16[1,2,1,8,512]{4,3,0,1,2:T(8,128)(2,1)S(1)}, u32[]{:S(2)}, u32[]{:S(2)}) collective-permute-start(bf16[1,2,1,8,512]{4,3,0,1,2:T(8,128)(2,1)S(1)} %get-tuple-element.22), channel_id=1, source_target_pairs={{0,8},{8,16},{16,24},{24,32},{32,40},{40,48},{48,56},{56,64},{64,7... | collective-permute-start | bytes 49160 | tf_op jit(solution)/shard_map/ppermute | solution.py:31
  172.0 10.1 %collective-permute-start.1 = (bf16[1,2,1,8,512]{4,3,0,1,2:T(8,128)(2,1)S(1)}, bf16[1,2,1,8,512]{4,3,0,1,2:T(8,128)(2,1)S(1)}, u32[]{:S(2)}, u32[]{:S(2)}) collective-permute-start(bf16[1,2,1,8,512]{4,3,0,1,2:T(8,128)(2,1)S(1)} %get-tuple-element.21), channel_id=1, source_target_pairs={{0,16},{8,24},{16,32},{24,40},{32,48},{40,56},{48,64},{56,72},{64,... | collective-permute-start | bytes 49160 | tf_op jit(solution)/shard_map/ppermute | solution.py:31
  174.5 9.2 %collective-permute-start.2 = (bf16[1,2,1,8,512]{4,3,0,1,2:T(8,128)(2,1)S(1)}, bf16[1,2,1,8,512]{4,3,0,1,2:T(8,128)(2,1)S(1)}, u32[]{:S(2)}, u32[]{:S(2)}) collective-permute-start(bf16[1,2,1,8,512]{4,3,0,1,2:T(8,128)(2,1)S(1)} %get-tuple-element.20), channel_id=1, source_target_pairs={{0,24},{8,32},{16,40},{24,48},{32,56},{40,64},{48,72},{56,80},{64,... | collective-permute-start | bytes 49160 | tf_op jit(solution)/shard_map/ppermute | solution.py:31
  175.3 10.4 %collective-permute-start.3 = (bf16[1,2,1,8,512]{4,3,0,1,2:T(8,128)(2,1)S(1)}, bf16[1,2,1,8,512]{4,3,0,1,2:T(8,128)(2,1)S(1)}, u32[]{:S(2)}, u32[]{:S(2)}) collective-permute-start(bf16[1,2,1,8,512]{4,3,0,1,2:T(8,128)(2,1)S(1)} %get-tuple-element.19), channel_id=1, source_target_pairs={{0,32},{8,40},{16,48},{24,56},{32,64},{40,72},{48,80},{56,88},{64,... | collective-permute-start | bytes 49160 | tf_op jit(solution)/shard_map/ppermute | solution.py:31
  176.5 11.1 %collective-permute-start.4 = (bf16[1,2,1,8,512]{4,3,0,1,2:T(8,128)(2,1)S(1)}, bf16[1,2,1,8,512]{4,3,0,1,2:T(8,128)(2,1)S(1)}, u32[]{:S(2)}, u32[]{:S(2)}) collective-permute-start(bf16[1,2,1,8,512]{4,3,0,1,2:T(8,128)(2,1)S(1)} %get-tuple-element.18), channel_id=1, source_target_pairs={{0,40},{8,48},{16,56},{24,64},{32,72},{40,80},{48,88},{56,96},{64,... | collective-permute-start | bytes 49160 | tf_op jit(solution)/shard_map/ppermute | solution.py:31
  180.3 11.3 %collective-permute-start.5 = (bf16[1,2,1,8,512]{4,3,0,1,2:T(8,128)(2,1)S(1)}, bf16[1,2,1,8,512]{4,3,0,1,2:T(8,128)(2,1)S(1)}, u32[]{:S(2)}, u32[]{:S(2)}) collective-permute-start(bf16[1,2,1,8,512]{4,3,0,1,2:T(8,128)(2,1)S(1)} %get-tuple-element.17), channel_id=1, source_target_pairs={{0,48},{8,56},{16,64},{24,72},{32,80},{40,88},{48,96},{56,104},{64... | collective-permute-start | bytes 49160 | tf_op jit(solution)/shard_map/ppermute | solution.py:31
  182.1 9.5 %collective-permute-start.6 = (bf16[1,2,1,8,512]{4,3,0,1,2:T(8,128)(2,1)S(1)}, bf16[1,2,1,8,512]{4,3,0,1,2:T(8,128)(2,1)S(1)}, u32[]{:S(2)}, u32[]{:S(2)}) collective-permute-start(bf16[1,2,1,8,512]{4,3,0,1,2:T(8,128)(2,1)S(1)} %get-tuple-element.16), channel_id=1, source_target_pairs={{0,56},{8,64},{16,72},{24,80},{32,88},{40,96},{48,104},{56,112},{6... | collective-permute-start | bytes 49160 | tf_op jit(solution)/shard_map/ppermute | solution.py:31
  183.7 8.6 %collective-permute-start.7 = (bf16[1,2,1,8,512]{4,3,0,1,2:T(8,128)(2,1)S(1)}, bf16[1,2,1,8,512]{4,3,0,1,2:T(8,128)(2,1)S(1)}, u32[]{:S(2)}, u32[]{:S(2)}) collective-permute-start(bf16[1,2,1,8,512]{4,3,0,1,2:T(8,128)(2,1)S(1)} %get-tuple-element.15), channel_id=1, source_target_pairs={{0,64},{8,72},{16,80},{24,88},{32,96},{40,104},{48,112},{56,120},{... | collective-permute-start | bytes 49160 | tf_op jit(solution)/shard_map/ppermute | solution.py:31
  185.7 12.5 %collective-permute-start.8 = (bf16[1,2,1,8,512]{4,3,0,1,2:T(8,128)(2,1)S(1)}, bf16[1,2,1,8,512]{4,3,0,1,2:T(8,128)(2,1)S(1)}, u32[]{:S(2)}, u32[]{:S(2)}) collective-permute-start(bf16[1,2,1,8,512]{4,3,0,1,2:T(8,128)(2,1)S(1)} %get-tuple-element.14), channel_id=1, source_target_pairs={{0,72},{8,80},{16,88},{24,96},{32,104},{40,112},{48,120},{56,0},{6... | collective-permute-start | bytes 49160 | tf_op jit(solution)/shard_map/ppermute | solution.py:31
  187.6 10.6 %collective-permute-start.9 = (bf16[1,2,1,8,512]{4,3,0,1,2:T(8,128)(2,1)S(1)}, bf16[1,2,1,8,512]{4,3,0,1,2:T(8,128)(2,1)S(1)}, u32[]{:S(2)}, u32[]{:S(2)}) collective-permute-start(bf16[1,2,1,8,512]{4,3,0,1,2:T(8,128)(2,1)S(1)} %get-tuple-element.13), channel_id=1, source_target_pairs={{0,80},{8,88},{16,96},{24,104},{32,112},{40,120},{48,0},{56,8},{64... | collective-permute-start | bytes 49160 | tf_op jit(solution)/shard_map/ppermute | solution.py:31
  191.6 7.5 %collective-permute-start.10 = (bf16[1,2,1,8,512]{4,3,0,1,2:T(8,128)(2,1)S(1)}, bf16[1,2,1,8,512]{4,3,0,1,2:T(8,128)(2,1)S(1)}, u32[]{:S(2)}, u32[]{:S(2)}) collective-permute-start(bf16[1,2,1,8,512]{4,3,0,1,2:T(8,128)(2,1)S(1)} %get-tuple-element.12), channel_id=1, source_target_pairs={{0,88},{8,96},{16,104},{24,112},{32,120},{40,0},{48,8},{56,16},{64... | collective-permute-start | bytes 49160 | tf_op jit(solution)/shard_map/ppermute | solution.py:31
  191.7 7.5 %collective-permute-start.11 = (bf16[1,2,1,8,512]{4,3,0,1,2:T(8,128)(2,1)S(1)}, bf16[1,2,1,8,512]{4,3,0,1,2:T(8,128)(2,1)S(1)}, u32[]{:S(2)}, u32[]{:S(2)}) collective-permute-start(bf16[1,2,1,8,512]{4,3,0,1,2:T(8,128)(2,1)S(1)} %get-tuple-element.11), channel_id=1, source_target_pairs={{0,96},{8,104},{16,112},{24,120},{32,0},{40,8},{48,16},{56,24},{64... | collective-permute-start | bytes 49160 | tf_op jit(solution)/shard_map/ppermute | solution.py:31
  192.3 7.3 %collective-permute-start.12 = (bf16[1,2,1,8,512]{4,3,0,1,2:T(8,128)(2,1)S(1)}, bf16[1,2,1,8,512]{4,3,0,1,2:T(8,128)(2,1)S(1)}, u32[]{:S(2)}, u32[]{:S(2)}) collective-permute-start(bf16[1,2,1,8,512]{4,3,0,1,2:T(8,128)(2,1)S(1)} %get-tuple-element.10), channel_id=1, source_target_pairs={{0,104},{8,112},{16,120},{24,0},{32,8},{40,16},{48,24},{56,32},{64... | collective-permute-start | bytes 49160 | tf_op jit(solution)/shard_map/ppermute | solution.py:31
  198.2 6.1 %collective-permute-start.13 = (bf16[1,2,1,8,512]{4,3,0,1,2:T(8,128)(2,1)S(1)}, bf16[1,2,1,8,512]{4,3,0,1,2:T(8,128)(2,1)S(1)}, u32[]{:S(2)}, u32[]{:S(2)}) collective-permute-start(bf16[1,2,1,8,512]{4,3,0,1,2:T(8,128)(2,1)S(1)} %get-tuple-element.9), channel_id=1, source_target_pairs={{0,112},{8,120},{16,0},{24,8},{32,16},{40,24},{48,32},{56,40},{64,... | collective-permute-start | bytes 49160 | tf_op jit(solution)/shard_map/ppermute | solution.py:31
  198.2 6.1 %collective-permute-start.14 = (bf16[1,2,1,8,512]{4,3,0,1,2:T(8,128)(2,1)S(1)}, bf16[1,2,1,8,512]{4,3,0,1,2:T(8,128)(2,1)S(1)}, u32[]{:S(2)}, u32[]{:S(2)}) collective-permute-start(bf16[1,2,1,8,512]{4,3,0,1,2:T(8,128)(2,1)S(1)} %get-tuple-element.8), channel_id=1, source_target_pairs={{0,120},{8,0},{16,8},{24,16},{32,24},{40,32},{48,40},{56,48},{64,5... | collective-permute-start | bytes 49160 | tf_op jit(solution)/shard_map/ppermute | solution.py:31
Sparse Core Ops, SparseCore 0:
  13.2 27.6 all-gather.3
  89.8 41.8 all-gather.5
  139.1 25.0 all-gather.7
